TPU v7x, 32 devices: a whole 2x2x4 slice. The times are simulated.
32 devices in a mesh: expert: 4 (over y, x), dp: 8 (over z, core).
Axes of the slice: x: 2, y: 2, z: 4, core: 2. Of those that a mesh axis runs over, the one named last changes fastest.
Arguments:
- hidden_rows: bfloat16 [4, 3072, 8192], P('expert', 'dp'), may hold values from -8 to 8
- out_grads: bfloat16 [4, 3072, 2048], P('expert', 'dp'), may hold values from -0.15625 to 0.15625
- counts: int32 [4, 8], P('expert', 'dp'), may hold values from 1 to 384, as said below
- expert_m: bfloat16 [4, 8192, 2048], P('expert', 'dp'), may hold values from -1.75 to 1.75
- expert_v: bfloat16 [4, 8192, 2048], P('expert', 'dp'), may hold values from 0.0029907227 to 0.029907227
- low_rank: bfloat16 [8192, 256], P(('expert', 'dp')), may hold values from -6 to 6
- dt_grads: bfloat16 [8192, 8192], P(('expert', 'dp')), may hold values from -0.0625 to 0.0625
- mamba_m: float32 [8192, 256], P(('expert', 'dp')), may hold values from -1.75 to 1.75
- mamba_v: float32 [8192, 256], P(('expert', 'dp')), may hold values from 0.003 to 0.03
Outputs:
- expert_m_new: bfloat16 [4, 8192, 2048], P('expert', 'dp')
- expert_v_new: bfloat16 [4, 8192, 2048], P('expert', 'dp')
- expert_step: bfloat16 [4, 8192, 2048], P('expert', 'dp')
- mamba_m_new: float32 [8192, 256], P(('expert', 'dp'))
- mamba_v_new: float32 [8192, 256], P(('expert', 'dp'))
- mamba_step: float32 [8192, 256], P(('expert', 'dp'))
Inputs may be any that keep to these rules, and one draw needn't show every extreme that they name: counts[e, d] is the number of live rows at the front of the 384 slots of block d of expert e; some block of every draw is full.
All inputs are finite; a program needn't handle non-finite values.
Results may differ from a plain program's by a relative error of at most 0.006.
Values may be sent and summed in bfloat16 or wider, within the bound.
A program may use at most 192 MiB of HBM per device.

v0:
```python
import jax
import jax.numpy as jnp
from jax import lax
from jax.sharding import PartitionSpec as P

STEP = 20


def adam_update(moment_old, second_old, gradient):
    moment_one = 0.9 * moment_old.astype(jnp.float32) + 0.1 * gradient
    second = 0.999 * second_old.astype(jnp.float32) + 0.001 * gradient * gradient
    direction = moment_one / (1.0 - 0.9**STEP) / (jnp.sqrt(second / (1.0 - 0.999**STEP)) + 1e-08)
    return (moment_one, second, direction)


def body(hidden_rows, out_grads, counts, expert_m, expert_v, low_rank, dt_grads, mamba_m, mamba_v):
    hidden = hidden_rows[0]
    out_rows = out_grads[0]
    capacity = hidden.shape[0]
    live_rows = counts[0, 0]
    positions = lax.broadcasted_iota(jnp.int32, (capacity, 1), 0)
    masked = jnp.where(positions < live_rows, out_rows, jnp.zeros_like(out_rows))
    contract = (((0,), (0,)), ((), ()))
    expert_grad = lax.psum_scatter(
        lax.dot_general(hidden, masked, contract, preferred_element_type=jnp.float32).astype(
            jnp.bfloat16
        ),
        "dp",
        scatter_dimension=0,
        tiled=True,
    ).astype(jnp.float32)
    moment_one, second, direction = adam_update(expert_m[0], expert_v[0], expert_grad)
    mamba_grad = lax.psum_scatter(
        lax.dot_general(dt_grads, low_rank, contract, preferred_element_type=jnp.float32),
        ("expert", "dp"),
        scatter_dimension=0,
        tiled=True,
    )
    mamba_one, mamba_two, mamba_dir = adam_update(mamba_m, mamba_v, mamba_grad)
    return (
        moment_one.astype(jnp.bfloat16)[None],
        second.astype(jnp.bfloat16)[None],
        direction.astype(jnp.bfloat16)[None],
        mamba_one,
        mamba_two,
        mamba_dir,
    )


def solution(mesh):
    in_specs = (
        P("expert", "dp", None),
        P("expert", "dp", None),
        P("expert", "dp"),
        P("expert", "dp", None),
        P("expert", "dp", None),
        P(("expert", "dp"), None),
        P(("expert", "dp"), None),
        P(("expert", "dp"), None),
        P(("expert", "dp"), None),
    )
    out_specs = (
        P("expert", "dp", None),
        P("expert", "dp", None),
        P("expert", "dp", None),
        P(("expert", "dp"), None),
        P(("expert", "dp"), None),
        P(("expert", "dp"), None),
    )
    return jax.shard_map(body, mesh=mesh, in_specs=in_specs, out_specs=out_specs, check_vma=False)
```

profile of v0, /device:TPU:0, one launch (start us, length us, event | category | flops | bytes accessed | tf_op | source)
XLA Modules:
  0.0 533.9 jit_solution(7335241494354486204)
XLA Ops:
  7.2 0.0 copy-start
  7.2 0.0 reduce-scatter.5.cloned.1.call-start
  7.2 0.8 copy-done
  8.1 6.7 %fusion.15 = f32[8192,256]{1,0:T(8,128)} fusion(bf16[256,8192]{1,0:T(8,128)(2,1)} %param.15, bf16[256,256]{1,0:T(8,128)(2,1)S(1)} %copy-done), kind=kOutput, calls=%fused_computation.22 | convolution fusion | flops 1073741824 | bytes 12713984 | tf_op jit(solution)/shard_map/dot_general | solution.py:34
  14.8 0.0 copy-start.4
  14.8 0.0 reduce-scatter.5.cloned.1.call-update
  14.8 0.0 reduce-scatter.3.cloned.1.call-start
  15.6 0.6 copy-done.4
  16.2 24.6 %convert_bitcast_fusion = bf16[8192,2048]{0,1:T(8,128)(2,1)} fusion(bf16[1,384,8192]{2,1,0:T(8,128)(2,1)} %param.9, bf16[1,384,2048]{2,1,0:T(8,128)(2,1)S(1)} %copy-done.4, pred[384]{0:T(512)(128)(4,1)S(1)} %iota_compare_fusion), kind=kOutput, calls=%fused_computation | convolution fusion | flops 12902465536 | bytes 41419136 | tf_op jit(solution)/shard_map/dot_general | solution.py:25
  40.9 0.0 reduce-scatter.3.cloned.1.call-update
  40.9 6.4 %copy.15 = bf16[1,1024,2048]{1,2,0:T(8,128)(2,1)} copy(bf16[1,1024,2048]{2,1,0:T(8,128)(2,1)} %param.12) | data formatting | bytes 8388608 | tf_op args[3]
  47.3 0.0 copy-start.2
  47.3 0.0 copy-start.3
  47.3 6.5 %copy.16 = bf16[1,1024,2048]{1,2,0:T(8,128)(2,1)} copy(bf16[1,1024,2048]{2,1,0:T(8,128)(2,1)} %param.13) | data formatting | bytes 8388608 | tf_op args[4]
  53.8 115.9 %reduce-scatter.5.cloned.1.call-done = f32[256,256]{1,0:T(8,128)} async-done(((f32[8192,256]{1,0:T(8,128)}), f32[256,256]{1,0:T(8,128)}) %reduce-scatter.5.cloned.1.call-update) | async-done | bytes 262160 | tf_op jit(solution)/shard_map/reduce_scatter | solution.py:33
  169.7 0.0 copy-done.2
  169.7 0.0 copy-done.3
  169.7 1.9 add_divide_fusion
  171.6 323.6 %reduce-scatter.3.cloned.1.call-done = bf16[1024,2048]{0,1:T(8,128)(2,1)} async-done(((bf16[8192,2048]{0,1:T(8,128)(2,1)}), bf16[1024,2048]{0,1:T(8,128)(2,1)}) %reduce-scatter.3.cloned.1.call-update) | async-done | bytes 4194320 | tf_op jit(solution)/shard_map/reduce_scatter | solution.py:24
  495.2 12.6 %fusion.7 = (bf16[1,1024,2048]{1,2,0:T(8,128)(2,1)}, bf16[1,1024,2048]{1,2,0:T(8,128)(2,1)}, bf16[1,1024,2048]{1,2,0:T(8,128)(2,1)}) fusion(bf16[1,1024,2048]{1,2,0:T(8,128)(2,1)} %copy.16, bf16[1024,2048]{0,1:T(8,128)(2,1)} %reduce-scatter.3.cloned.1.call-done, bf16[1,1024,2048]{1,2,0:T(8,128)(2,1)} %copy.15), kind=kLoop, calls=%fused_computation.11 | loop fusion | flops 35651584 | bytes 25165824 | tf_op jit(solution)/shard_map/broadcast_in_dim | solution.py:43
  507.8 6.4 %copy.17 = bf16[1,1024,2048]{2,1,0:T(8,128)(2,1)} copy(bf16[1,1024,2048]{1,2,0:T(8,128)(2,1)} %get-tuple-element.16) | data formatting | bytes 8388608
  514.2 0.0 copy-start.1
  514.2 6.5 %copy.18 = bf16[1,1024,2048]{2,1,0:T(8,128)(2,1)} copy(bf16[1,1024,2048]{1,2,0:T(8,128)(2,1)} %get-tuple-element.17) | data formatting | bytes 8388608
  520.6 6.4 %copy.19 = bf16[1,1024,2048]{2,1,0:T(8,128)(2,1)} copy(bf16[1,1024,2048]{1,2,0:T(8,128)(2,1)} %get-tuple-element.15) | data formatting | bytes 8388608
  527.1 0.0 copy-done.1
  (1 shorter events, 0.0 us)
Async XLA Ops:
  7.2 0.9 copy-start
  7.2 162.5 %reduce-scatter.5.cloned.1.call-start = ((), (), s32[]{:S(2)}) async-start(), calls=%async_computation.3 | async-start | bytes 8650752 | tf_op jit(solution)/shard_map/reduce_scatter | solution.py:33
  14.8 1.4 copy-start.4
  14.8 480.4 %reduce-scatter.3.cloned.1.call-start = ((), (), s32[]{:S(2)}) async-start(), calls=%async_computation.2 | async-start | bytes 37748736 | tf_op jit(solution)/shard_map/reduce_scatter | solution.py:24
  47.3 122.4 %copy-start.2 = (f32[256,256]{1,0:T(8,128)S(1)}, f32[256,256]{1,0:T(8,128)}, u32[]{:S(2)}) copy-start(f32[256,256]{1,0:T(8,128)} %param.17) | copy-start | bytes 786436
  47.3 122.4 %copy-start.3 = (f32[256,256]{1,0:T(8,128)S(1)}, f32[256,256]{1,0:T(8,128)}, u32[]{:S(2)}) copy-start(f32[256,256]{1,0:T(8,128)} %param.16) | copy-start | bytes 786436
  514.2 12.9 %copy-start.1 = (bf16[256,256]{1,0:T(8,128)(2,1)S(1)}, bf16[256,256]{1,0:T(8,128)(2,1)}, u32[]{:S(2)}) copy-start(bf16[256,256]{1,0:T(8,128)(2,1)} %param.14) | copy-start | bytes 393220
Sparse Core Ops, SparseCore 0:
  14.9 154.7 reduce-scatter.4
  172.1 323.0 reduce-scatter.2
where the time goes:
time: 535 us; the launch traced here: 534 us
  waiting for transfers between devices  440 us (82%)
  local copies, waits for them, and re-layouts  33.6 us (6%)
  matrix products  31.4 us (6%)
  between operations  14.8 us (3%)
  other arithmetic  14.5 us (3%)
    reduce_scatter x1, waiting for transfers between devices, body(): lax.psum_scatter(lax.dot_general(hidden, masked, contract, preferred_elem...  324 us
    reduce_scatter x1, waiting for transfers between devices, body(): lax.psum_scatter(lax.dot_general(dt_grads, low_rank, contract, preferred_...  116 us
    unnamed x15, local copies, waits for them, and re-layouts  33.6 us
    dot_general x1, matrix products, body(): lax.dot_general(hidden, masked, contract, preferred_element_type=jnp.floa...  24.6 us
    broadcast_in_dim x1, other arithmetic, body(): direction.astype(jnp.bfloat16)[None]  12.6 us
  transfers between devices with their start and end apart: 2, of which 2 were waited for; matrix products, arithmetic and copies ran while one was open for 7% of the time, Pallas kernels for 0%

commit v1 on v0

v1 whole, which is shorter than its diff:
```python
import functools

import jax
import jax.numpy as jnp
from jax import lax
from jax.experimental import pallas as pl
from jax.experimental.pallas import tpu as pltpu
from jax.sharding import PartitionSpec as P

STEP = 20
MESH = pl.DeviceIdType.MESH


def adam_update(moment_old, second_old, gradient):
    moment_one = 0.9 * moment_old.astype(jnp.float32) + 0.1 * gradient
    second = 0.999 * second_old.astype(jnp.float32) + 0.001 * gradient * gradient
    direction = moment_one / (1.0 - 0.9**STEP) / (jnp.sqrt(second / (1.0 - 0.999**STEP)) + 1e-08)
    return (moment_one, second, direction)


def expert_kernel(
    n, count_ref, h_ref, o_ref, acc, hid, outs, hid_send, hid_recv, line_send, sib_send, out_recv, own_sem
):
    chips = n // 2
    d = lax.axis_index("dp")
    p, c = d // 2, d % 2
    sibling = 2 * p + 1 - c
    capacity = o_ref.shape[0]
    cols = hid.shape[2]

    def columns(t):
        return pl.ds(pl.multiple_of(t * cols, cols), cols)

    own = pltpu.make_async_copy(h_ref.at[:, columns(d)], hid.at[d], own_sem)
    own.start()
    positions = lax.broadcasted_iota(jnp.int32, o_ref.shape, 0)
    value = o_ref[...]
    outs[d] = jnp.where(positions < count_ref[0, 0], value, jnp.zeros_like(value))

    barrier = pltpu.get_barrier_semaphore()
    for k in range(1, n):
        pl.semaphore_signal(barrier, inc=1, device_id={"dp": (d + k) % n}, device_id_type=MESH)
    pl.semaphore_wait(barrier, n - 1)

    def line_copy(side, q):
        s = 2 * q + c
        return pltpu.make_async_remote_copy(
            src_ref=outs.at[s],
            dst_ref=outs.at[s],
            send_sem=line_send.at[side, q],
            recv_sem=out_recv.at[s],
            device_id={"dp": d + (2 if side else -2)},
            device_id_type=MESH,
        )

    def sib_copy(q):
        s = 2 * q + c
        return pltpu.make_async_remote_copy(
            src_ref=outs.at[s],
            dst_ref=outs.at[s],
            send_sem=sib_send.at[q],
            recv_sem=out_recv.at[s],
            device_id={"dp": sibling},
            device_id_type=MESH,
        )

    def out_arrival(s):
        return pltpu.make_async_copy(outs.at[s], outs.at[s], out_recv.at[s])

    def hid_copy(t):
        return pltpu.make_async_remote_copy(
            src_ref=h_ref.at[:, columns(t)],
            dst_ref=hid.at[d],
            send_sem=hid_send.at[t],
            recv_sem=hid_recv.at[d],
            device_id={"dp": t},
            device_id_type=MESH,
        )

    def hid_arrival(s):
        return pltpu.make_async_copy(hid.at[s], hid.at[s], hid_recv.at[s])

    @pl.when(p < chips - 1)
    def _():
        line_copy(1, p).start()

    @pl.when(p > 0)
    def _():
        line_copy(0, p).start()

    sib_copy(p).start()
    hid_copy(sibling).start()
    for k in range(1, chips):
        for sign in (-1, 1):
            q = p + sign * k

            @pl.when(jnp.logical_and(q >= 0, q < chips))
            def _(q=q):
                hid_copy(2 * q + c).start()
                hid_copy(2 * q + 1 - c).start()

    acc[...] = jnp.zeros_like(acc)

    rows = min(256, cols)
    width = 512

    def multiply(s):
        @pl.loop(0, cols // rows)
        def _(i):
            at = pl.ds(pl.multiple_of(i * rows, rows), rows)
            left = hid[s, :, at]

            for j in range(acc.shape[1] // width):
                wide = pl.ds(j * width, width)
                acc[at, wide] += lax.dot_general(
                    left,
                    outs[s, :, wide],
                    (((0,), (0,)), ((), ())),
                    preferred_element_type=jnp.float32,
                )

    def forward(k):
        left, right = p - k, p + k

        @pl.when(left >= 0)
        def _():
            out_arrival(2 * left + c).wait()

            @pl.when(p < chips - 1)
            def _():
                line_copy(1, left).start()

            sib_copy(left).start()

        @pl.when(right < chips)
        def _():
            out_arrival(2 * right + c).wait()

            @pl.when(p > 0)
            def _():
                line_copy(0, right).start()

            sib_copy(right).start()

    def multiply_at(k):
        @pl.loop(0, 4)
        def _(j):
            q = p + (2 * (j // 2) - 1) * k
            cc = (c + j) % 2

            @pl.when(jnp.logical_and(q >= 0, q < chips))
            def _():
                s = 2 * q + cc

                @pl.when(cc != c)
                def _():
                    out_arrival(s).wait()

                hid_arrival(s).wait()
                multiply(s)

    own.wait()
    multiply(d)
    out_arrival(sibling).wait()
    hid_arrival(sibling).wait()
    multiply(sibling)

    @pl.loop(1, chips + 1)
    def _(k):
        @pl.when(k < chips)
        def _():
            forward(k)

        @pl.when(k > 1)
        def _():
            multiply_at(k - 1)

    @pl.loop(0, chips)
    def _(q):
        sib_copy(q).wait_send()

        @pl.when(jnp.logical_and(q <= p, p < chips - 1))
        def _():
            line_copy(1, q).wait_send()

        @pl.when(jnp.logical_and(q >= p, p > 0))
        def _():
            line_copy(0, q).wait_send()

    @pl.loop(1, n)
    def _(k):
        hid_copy((d + k) % n).wait_send()


def expert_gradient(n, counts, hidden, out_rows):
    capacity, total = hidden.shape
    width = out_rows.shape[1]
    cols = total // n
    chips = n // 2
    return pl.pallas_call(
        functools.partial(expert_kernel, n),
        out_shape=jax.ShapeDtypeStruct((cols, width), jnp.float32),
        in_specs=[
            pl.BlockSpec(memory_space=pltpu.SMEM),
            pl.BlockSpec(memory_space=pl.ANY),
            pl.BlockSpec(memory_space=pltpu.VMEM),
        ],
        out_specs=pl.BlockSpec(memory_space=pltpu.VMEM),
        scratch_shapes=[
            pltpu.VMEM((n, capacity, cols), jnp.bfloat16),
            pltpu.VMEM((n, capacity, width), jnp.bfloat16),
            pltpu.SemaphoreType.DMA((n,)),
            pltpu.SemaphoreType.DMA((n,)),
            pltpu.SemaphoreType.DMA((2, chips)),
            pltpu.SemaphoreType.DMA((chips,)),
            pltpu.SemaphoreType.DMA((n,)),
            pltpu.SemaphoreType.DMA,
        ],
        compiler_params=pltpu.CompilerParams(
            collective_id=0, has_side_effects=True, vmem_limit_bytes=52 * 2**20
        ),
        cost_estimate=pl.CostEstimate(
            flops=2 * n * capacity * cols * width, bytes_accessed=600 * 2**20, transcendentals=0
        ),
    )(counts, hidden, out_rows)


def body(n, hidden_rows, out_grads, counts, expert_m, expert_v, low_rank, dt_grads, mamba_m, mamba_v):
    contract = (((0,), (0,)), ((), ()))
    mamba_grad = lax.psum_scatter(
        lax.dot_general(dt_grads, low_rank, contract, preferred_element_type=jnp.float32).astype(
            jnp.bfloat16
        ),
        ("expert", "dp"),
        scatter_dimension=0,
        tiled=True,
    ).astype(jnp.float32)
    expert_grad = expert_gradient(n, counts, hidden_rows[0], out_grads[0])
    moment_one, second, direction = adam_update(expert_m[0], expert_v[0], expert_grad)
    mamba_one, mamba_two, mamba_dir = adam_update(mamba_m, mamba_v, mamba_grad)
    return (
        moment_one.astype(jnp.bfloat16)[None],
        second.astype(jnp.bfloat16)[None],
        direction.astype(jnp.bfloat16)[None],
        mamba_one,
        mamba_two,
        mamba_dir,
    )


def solution(mesh):
    in_specs = (
        P("expert", "dp", None),
        P("expert", "dp", None),
        P("expert", "dp"),
        P("expert", "dp", None),
        P("expert", "dp", None),
        P(("expert", "dp"), None),
        P(("expert", "dp"), None),
        P(("expert", "dp"), None),
        P(("expert", "dp"), None),
    )
    out_specs = (
        P("expert", "dp", None),
        P("expert", "dp", None),
        P("expert", "dp", None),
        P(("expert", "dp"), None),
        P(("expert", "dp"), None),
        P(("expert", "dp"), None),
    )
    return jax.shard_map(
        functools.partial(body, mesh.shape["dp"]),
        mesh=mesh,
        in_specs=in_specs,
        out_specs=out_specs,
        check_vma=False,
    )
```

time: 535 us -> 338 us (0.63)
  waiting for transfers between devices: 440 us -> 0.02 us
  Pallas kernels: 0 us -> 303 us
  local copies, waits for them, and re-layouts: 33.6 us -> 0.88 us
  matrix products: 31.4 us -> 5.46 us
    reduce_scatter x1 -> x0, waiting for transfers between devices: 324 us -> none  [body(): lax.psum_scatter(lax.dot_general(hidden, masked, contract, preferred_elem...]
    pallas_call x0 -> x1, Pallas kernels: none -> 303 us  [expert_gradient(): pl.pallas_call(functools.partial(expert_kernel, n), out_shape=jax.ShapeDt...]
    reduce_scatter x1, waiting for transfers between devices: 116 us -> 0.01 us  [body(): lax.psum_scatter(lax.dot_general(dt_grads, low_rank, contract, preferred_...]
    unnamed x15 -> x12, local copies, waits for them, and re-layouts: 33.6 us -> 0.88 us
    dot_general x1 -> x0, matrix products: 24.6 us -> none  [body(): lax.dot_general(hidden, masked, contract, preferred_element_type=jnp.floa...]
  transfers between devices with their start and end apart: 2 -> 1, of which waited for: 2 -> 0; matrix products, arithmetic and copies ran while one was open for 7% -> 3% of each run, Pallas kernels for 0% -> 90%
where the time goes in v1:
time: 338 us; the launch traced here: 337 us
  Pallas kernels  303 us (90%)
  between operations  14.8 us (4%)
  other arithmetic  13.2 us (4%)
  matrix products  5.46 us (2%)
    pallas_call x1, Pallas kernels, expert_gradient(): pl.pallas_call(functools.partial(expert_kernel, n), out_shape=jax.ShapeDt...  303 us
    broadcast_in_dim x1, other arithmetic, body(): direction.astype(jnp.bfloat16)[None]  11.3 us
  transfers between devices with their start and end apart: 1, of which 0 were waited for; matrix products, arithmetic and copies ran while one was open for 3% of the time, Pallas kernels for 90%

profile of v1, /device:TPU:0, one launch (start us, length us, event | category | flops | bytes accessed | tf_op | source)
XLA Modules:
  0.0 337.4 jit_solution(14579563683052131772)
XLA Ops:
  7.2 0.0 copy-start
  7.2 0.0 copy-start.1
  7.2 0.0 reduce-scatter.2.cloned.1.call-start
  7.2 0.8 copy-done
  8.1 5.5 %convolution_convert_fusion = bf16[8192,256]{1,0:T(8,128)(2,1)} fusion(bf16[256,8192]{1,0:T(8,128)(2,1)} %param.15, bf16[256,256]{1,0:T(8,128)(2,1)S(1)} %copy-done), kind=kOutput, calls=%fused_computation.1 | convolution fusion | flops 1075838976 | bytes 8519680 | tf_op jit(solution)/shard_map/dot_general | solution.py:231
  13.5 0.0 reduce-scatter.2.cloned.1.call-update
  14.2 0.0 copy-done.1
  14.2 0.0 copy-start.2
  14.2 0.0 copy-start.3
  14.2 303.1 %shard_map.136 = f32[1024,2048]{1,0:T(8,128)} custom-call(s32[1,1]{1,0:T(1,128)S(6)} %copy.15.count_ref, bf16[384,8192]{1,0:T(8,128)(2,1)} %bitcast.31, bf16[384,2048]{1,0:T(8,128)(2,1)S(1)} %bitcast.30), custom_call_target="tpu_custom_call" | custom-call | flops 12884901888 | bytes 629145600 | tf_op jit(solution)/shard_map/pallas_call | solution.py:200
  317.3 0.0 copy-done.2
  317.3 0.0 copy-done.3
  317.3 0.0 copy-start.4
  317.4 0.0 copy-start.5
  317.4 11.3 %fusion.5 = (bf16[1,1024,2048]{2,1,0:T(8,128)(2,1)}, bf16[1,1024,2048]{2,1,0:T(8,128)(2,1)}, bf16[1,1024,2048]{2,1,0:T(8,128)(2,1)}) fusion(f32[1024,2048]{1,0:T(8,128)} %shard_map.136, bf16[1,1024,2048]{2,1,0:T(8,128)(2,1)S(1)} %copy-done.2, bf16[1,1024,2048]{2,1,0:T(8,128)(2,1)S(1)} %copy-done.3), kind=kLoop, calls=%fused_computation.9 | loop fusion | flops 33554432 | bytes 29360128 | tf_op jit(solution)/shard_map/broadcast_in_dim | solution.py:244
  328.7 0.0 reduce-scatter.2.cloned.1.call-done
  328.7 0.0 copy-done.4
  328.7 0.0 copy-done.5
  328.7 1.9 add_divide_fusion
Async XLA Ops:
  7.2 0.9 copy-start
  7.2 7.0 %copy-start.1 = (bf16[1,384,2048]{2,1,0:T(8,128)(2,1)S(1)}, bf16[1,384,2048]{2,1,0:T(8,128)(2,1)}, u32[]{:S(2)}) copy-start(bf16[1,384,2048]{2,1,0:T(8,128)(2,1)} %param.10) | copy-start | bytes 4718596
  7.2 321.5 %reduce-scatter.2.cloned.1.call-start = ((), (), s32[]{:S(2)}) async-start(), calls=%async_computation.1 | async-start | bytes 4325376 | tf_op jit(solution)/shard_map/reduce_scatter | solution.py:230
  14.2 303.1 %copy-start.2 = (bf16[1,1024,2048]{2,1,0:T(8,128)(2,1)S(1)}, bf16[1,1024,2048]{2,1,0:T(8,128)(2,1)}, u32[]{:S(2)}) copy-start(bf16[1,1024,2048]{2,1,0:T(8,128)(2,1)} %param.13) | copy-start | bytes 12582916
  14.2 303.1 %copy-start.3 = (bf16[1,1024,2048]{2,1,0:T(8,128)(2,1)S(1)}, bf16[1,1024,2048]{2,1,0:T(8,128)(2,1)}, u32[]{:S(2)}) copy-start(bf16[1,1024,2048]{2,1,0:T(8,128)(2,1)} %param.12) | copy-start | bytes 12582916
  317.3 11.3 %copy-start.4 = (f32[256,256]{1,0:T(8,128)S(1)}, f32[256,256]{1,0:T(8,128)}, u32[]{:S(2)}) copy-start(f32[256,256]{1,0:T(8,128)} %param.17) | copy-start | bytes 786436
  317.4 11.3 %copy-start.5 = (f32[256,256]{1,0:T(8,128)S(1)}, f32[256,256]{1,0:T(8,128)}, u32[]{:S(2)}) copy-start(f32[256,256]{1,0:T(8,128)} %param.16) | copy-start | bytes 786436
Sparse Core Ops, SparseCore 0:
  13.7 210.5 reduce-scatter.1

commit v2 on v1

--- a/solution.py
+++ b/solution.py
@@ -19,10 +19,37 @@
 
 
 def expert_kernel(
-    n, count_ref, h_ref, o_ref, acc, hid, outs, hid_send, hid_recv, line_send, sib_send, out_recv, own_sem
+    n,
+    groups,
+    count_ref,
+    h_ref,
+    o_ref,
+    g_ref,
+    acc,
+    total,
+    hid,
+    outs,
+    first,
+    first_sum,
+    second,
+    second_sum,
+    third,
+    hid_send,
+    hid_recv,
+    line_send,
+    sib_send,
+    out_recv,
+    own_sem,
+    first_send,
+    first_recv,
+    second_send,
+    second_recv,
+    third_send,
+    third_recv,
 ):
     chips = n // 2
     d = lax.axis_index("dp")
+    e = lax.axis_index("expert")
     p, c = d // 2, d % 2
     sibling = 2 * p + 1 - c
     capacity = o_ref.shape[0]
@@ -40,7 +67,11 @@
     barrier = pltpu.get_barrier_semaphore()
     for k in range(1, n):
         pl.semaphore_signal(barrier, inc=1, device_id={"dp": (d + k) % n}, device_id_type=MESH)
-    pl.semaphore_wait(barrier, n - 1)
+    for k in range(1, groups):
+        pl.semaphore_signal(
+            barrier, inc=1, device_id={"expert": (e + k) % groups}, device_id_type=MESH
+        )
+    pl.semaphore_wait(barrier, n + groups - 2)
 
     def line_copy(side, q):
         s = 2 * q + c
@@ -80,6 +111,79 @@
     def hid_arrival(s):
         return pltpu.make_async_copy(hid.at[s], hid.at[s], hid_recv.at[s])
 
+    span = g_ref.shape[0] // groups
+    block = total.shape[0]
+
+    def first_copy(t):
+        return pltpu.make_async_remote_copy(
+            src_ref=g_ref.at[pl.ds(pl.multiple_of(t * span, span), span), :],
+            dst_ref=first.at[e],
+            send_sem=first_send.at[t],
+            recv_sem=first_recv.at[e],
+            device_id={"expert": t},
+            device_id_type=MESH,
+        )
+
+    def second_copy():
+        return pltpu.make_async_remote_copy(
+            src_ref=first_sum.at[:, 1 - c],
+            dst_ref=second,
+            send_sem=second_send,
+            recv_sem=second_recv,
+            device_id={"dp": sibling},
+            device_id_type=MESH,
+        )
+
+    def third_copy(q):
+        return pltpu.make_async_remote_copy(
+            src_ref=second_sum.at[q],
+            dst_ref=third.at[p],
+            send_sem=third_send.at[q],
+            recv_sem=third_recv.at[p],
+            device_id={"dp": 2 * q + c},
+            device_id_type=MESH,
+        )
+
+    def arrival(buffer, sem, at):
+        return pltpu.make_async_copy(buffer.at[at], buffer.at[at], sem.at[at])
+
+    def finish_first():
+        for k in range(1, groups):
+            arrival(first, first_recv, (e + k) % groups).wait()
+
+        @pl.loop(0, n)
+        def _(t):
+            summed = g_ref[
+                pl.ds(pl.multiple_of(e * span + t * block, block), block), :
+            ].astype(jnp.float32)
+            for k in range(1, groups):
+                summed += first[
+                    (e + k) % groups, pl.ds(pl.multiple_of(t * block, block), block), :
+                ].astype(jnp.float32)
+            first_sum[t // 2, t % 2] = summed.astype(jnp.bfloat16)
+
+        second_copy().start()
+
+    def finish_second():
+        pltpu.make_async_copy(second, second, second_recv).wait()
+
+        @pl.loop(0, chips)
+        def _(q):
+            second_sum[q] = (
+                first_sum[q, c].astype(jnp.float32) + second[q].astype(jnp.float32)
+            ).astype(jnp.bfloat16)
+
+        for k in range(1, chips):
+            third_copy((p + k) % chips).start()
+
+    def finish_third():
+        summed = second_sum[p].astype(jnp.float32)
+        for k in range(1, chips):
+            q = (p + k) % chips
+            arrival(third, third_recv, q).wait()
+            summed += third[q].astype(jnp.float32)
+        total[...] = summed
+
     @pl.when(p < chips - 1)
     def _():
         line_copy(1, p).start()
@@ -88,9 +192,12 @@
     def _():
         line_copy(0, p).start()
 
+    for k in range(1, groups):
+        first_copy((e + k) % groups).start()
     sib_copy(p).start()
     hid_copy(sibling).start()
-    for k in range(1, chips):
+
+    def hid_start(k):
         for sign in (-1, 1):
             q = p + sign * k
 
@@ -98,6 +205,8 @@
             def _(q=q):
                 hid_copy(2 * q + c).start()
                 hid_copy(2 * q + 1 - c).start()
+
+    hid_start(1)
 
     acc[...] = jnp.zeros_like(acc)
 
@@ -171,9 +280,23 @@
         def _():
             forward(k)
 
+            @pl.when(k < chips - 1)
+            def _():
+                hid_start(k + 1)
+
+        @pl.when(k == 1)
+        def _():
+            finish_first()
+
+        @pl.when(k == 2)
+        def _():
+            finish_second()
+
         @pl.when(k > 1)
         def _():
             multiply_at(k - 1)
+
+    finish_third()
 
     @pl.loop(0, chips)
     def _(q):
@@ -191,30 +314,56 @@
     def _(k):
         hid_copy((d + k) % n).wait_send()
 
-
-def expert_gradient(n, counts, hidden, out_rows):
+    for k in range(1, groups):
+        first_copy((e + k) % groups).wait_send()
+    second_copy().wait_send()
+    for k in range(1, chips):
+        third_copy((p + k) % chips).wait_send()
+
+
+def gradients(n, groups, counts, hidden, out_rows, mamba_part):
     capacity, total = hidden.shape
     width = out_rows.shape[1]
     cols = total // n
     chips = n // 2
+    inner, rank = mamba_part.shape
+    block = inner // (n * groups)
     return pl.pallas_call(
-        functools.partial(expert_kernel, n),
-        out_shape=jax.ShapeDtypeStruct((cols, width), jnp.float32),
+        functools.partial(expert_kernel, n, groups),
+        out_shape=(
+            jax.ShapeDtypeStruct((cols, width), jnp.float32),
+            jax.ShapeDtypeStruct((block, rank), jnp.float32),
+        ),
         in_specs=[
             pl.BlockSpec(memory_space=pltpu.SMEM),
             pl.BlockSpec(memory_space=pl.ANY),
             pl.BlockSpec(memory_space=pltpu.VMEM),
+            pl.BlockSpec(memory_space=pltpu.VMEM),
         ],
-        out_specs=pl.BlockSpec(memory_space=pltpu.VMEM),
+        out_specs=(
+            pl.BlockSpec(memory_space=pltpu.VMEM),
+            pl.BlockSpec(memory_space=pltpu.VMEM),
+        ),
         scratch_shapes=[
             pltpu.VMEM((n, capacity, cols), jnp.bfloat16),
             pltpu.VMEM((n, capacity, width), jnp.bfloat16),
+            pltpu.VMEM((groups, inner // groups, rank), jnp.bfloat16),
+            pltpu.VMEM((chips, 2, block, rank), jnp.bfloat16),
+            pltpu.VMEM((chips, block, rank), jnp.bfloat16),
+            pltpu.VMEM((chips, block, rank), jnp.bfloat16),
+            pltpu.VMEM((chips, block, rank), jnp.bfloat16),
             pltpu.SemaphoreType.DMA((n,)),
             pltpu.SemaphoreType.DMA((n,)),
             pltpu.SemaphoreType.DMA((2, chips)),
             pltpu.SemaphoreType.DMA((chips,)),
             pltpu.SemaphoreType.DMA((n,)),
             pltpu.SemaphoreType.DMA,
+            pltpu.SemaphoreType.DMA((groups,)),
+            pltpu.SemaphoreType.DMA((groups,)),
+            pltpu.SemaphoreType.DMA,
+            pltpu.SemaphoreType.DMA,
+            pltpu.SemaphoreType.DMA((chips,)),
+            pltpu.SemaphoreType.DMA((chips,)),
         ],
         compiler_params=pltpu.CompilerParams(
             collective_id=0, has_side_effects=True, vmem_limit_bytes=52 * 2**20
@@ -222,20 +371,19 @@
         cost_estimate=pl.CostEstimate(
             flops=2 * n * capacity * cols * width, bytes_accessed=600 * 2**20, transcendentals=0
         ),
-    )(counts, hidden, out_rows)
-
-
-def body(n, hidden_rows, out_grads, counts, expert_m, expert_v, low_rank, dt_grads, mamba_m, mamba_v):
+    )(counts, hidden, out_rows, mamba_part)
+
+
+def body(
+    n, groups, hidden_rows, out_grads, counts, expert_m, expert_v, low_rank, dt_grads, mamba_m, mamba_v
+):
     contract = (((0,), (0,)), ((), ()))
-    mamba_grad = lax.psum_scatter(
-        lax.dot_general(dt_grads, low_rank, contract, preferred_element_type=jnp.float32).astype(
-            jnp.bfloat16
-        ),
-        ("expert", "dp"),
-        scatter_dimension=0,
-        tiled=True,
-    ).astype(jnp.float32)
-    expert_grad = expert_gradient(n, counts, hidden_rows[0], out_grads[0])
+    mamba_part = lax.dot_general(
+        dt_grads, low_rank, contract, preferred_element_type=jnp.float32
+    ).astype(jnp.bfloat16)
+    expert_grad, mamba_grad = gradients(
+        n, groups, counts, hidden_rows[0], out_grads[0], mamba_part
+    )
     moment_one, second, direction = adam_update(expert_m[0], expert_v[0], expert_grad)
     mamba_one, mamba_two, mamba_dir = adam_update(mamba_m, mamba_v, mamba_grad)
     return (
@@ -269,7 +417,7 @@
         P(("expert", "dp"), None),
     )
     return jax.shard_map(
-        functools.partial(body, mesh.shape["dp"]),
+        functools.partial(body, mesh.shape["dp"], mesh.shape["expert"]),
         mesh=mesh,
         in_specs=in_specs,
         out_specs=out_specs,

time: 338 us -> 290 us (0.86)
  Pallas kernels: 303 us -> 270 us
  between operations: 14.8 us -> 1.37 us
    pallas_call x1, Pallas kernels: 303 us -> 270 us  [gradients(): pl.pallas_call(functools.partial(expert_kernel, n, groups), out_shape=(ja...]
  transfers between devices with their start and end apart: 1 -> 0, of which waited for: 0 -> 0; matrix products, arithmetic and copies ran while one was open for 3% -> 0% of each run, Pallas kernels for 90% -> 0%
where the time goes in v2:
time: 290 us
  Pallas kernels  270 us (93%)
  other arithmetic  12.3 us (4%)
  matrix products  5.51 us (2%)
    pallas_call x1, Pallas kernels, gradients(): pl.pallas_call(functools.partial(expert_kernel, n, groups), out_shape=(ja...  270 us
    broadcast_in_dim x1, other arithmetic, body(): direction.astype(jnp.bfloat16)[None]  11.3 us

profile of v2, /device:TPU:0, one launch (start us, length us, event | category | flops | bytes accessed | tf_op | source)
XLA Modules:
  0.0 290.0 jit_solution(715991452538469727)
XLA Ops:
  0.6 0.0 copy-start
  0.6 0.0 copy-start.1
  0.7 0.9 copy-done
  1.5 5.5 %convolution_convert_fusion.g_ref = bf16[8192,256]{1,0:T(8,128)(2,1)} fusion(bf16[256,8192]{1,0:T(8,128)(2,1)} %param.15, bf16[256,256]{1,0:T(8,128)(2,1)S(1)} %copy-done), kind=kOutput, calls=%fused_computation.1 | convolution fusion | flops 1075838976 | bytes 8519680 | tf_op jit(solution)/shard_map/dot_general | solution.py:381
  7.7 0.0 copy-done.1
  7.7 0.0 copy-start.2
  7.7 0.0 copy-start.3
  7.7 269.9 %shard_map.136 = (f32[1024,2048]{1,0:T(8,128)}, f32[256,256]{1,0:T(8,128)S(1)}) custom-call(s32[1,1]{1,0:T(1,128)S(6)} %copy.15.count_ref, bf16[384,8192]{1,0:T(8,128)(2,1)} %bitcast.31, bf16[384,2048]{1,0:T(8,128)(2,1)S(1)} %bitcast.30, bf16[8192,256]{1,0:T(8,128)(2,1)} %convolution_convert_fusion.g_ref), custom_call_target="tpu_custom_call" | custom-call | flops 12884901888 | bytes 629145600 | tf_op jit(solution)/shard_map/pallas_call | solution.py:331
  277.7 0.0 copy-done.2
  277.7 0.0 copy-done.3
  277.7 0.0 copy-start.4
  277.7 0.0 copy-start.5
  277.7 11.3 %fusion.5 = (bf16[1,1024,2048]{2,1,0:T(8,128)(2,1)}, bf16[1,1024,2048]{2,1,0:T(8,128)(2,1)}, bf16[1,1024,2048]{2,1,0:T(8,128)(2,1)}) fusion(f32[1024,2048]{1,0:T(8,128)} %get-tuple-element.8, bf16[1,1024,2048]{2,1,0:T(8,128)(2,1)S(1)} %copy-done.2, bf16[1,1024,2048]{2,1,0:T(8,128)(2,1)S(1)} %copy-done.3), kind=kLoop, calls=%fused_computation.9 | loop fusion | flops 33554432 | bytes 29360128 | tf_op jit(solution)/shard_map/broadcast_in_dim | solution.py:392
  289.0 0.0 copy-done.4
  289.0 0.0 copy-done.5
  289.0 1.0 add_divide_fusion
Async XLA Ops:
  0.6 0.9 copy-start
  0.6 7.1 %copy-start.1 = (bf16[1,384,2048]{2,1,0:T(8,128)(2,1)S(1)}, bf16[1,384,2048]{2,1,0:T(8,128)(2,1)}, u32[]{:S(2)}) copy-start(bf16[1,384,2048]{2,1,0:T(8,128)(2,1)} %param.10) | copy-start | bytes 4718596
  7.7 270.0 %copy-start.2 = (bf16[1,1024,2048]{2,1,0:T(8,128)(2,1)S(1)}, bf16[1,1024,2048]{2,1,0:T(8,128)(2,1)}, u32[]{:S(2)}) copy-start(bf16[1,1024,2048]{2,1,0:T(8,128)(2,1)} %param.13) | copy-start | bytes 12582916
  7.7 270.0 %copy-start.3 = (bf16[1,1024,2048]{2,1,0:T(8,128)(2,1)S(1)}, bf16[1,1024,2048]{2,1,0:T(8,128)(2,1)}, u32[]{:S(2)}) copy-start(bf16[1,1024,2048]{2,1,0:T(8,128)(2,1)} %param.12) | copy-start | bytes 12582916
  277.7 11.3 %copy-start.4 = (f32[256,256]{1,0:T(8,128)S(1)}, f32[256,256]{1,0:T(8,128)}, u32[]{:S(2)}) copy-start(f32[256,256]{1,0:T(8,128)} %param.17) | copy-start | bytes 786436
  277.7 11.3 %copy-start.5 = (f32[256,256]{1,0:T(8,128)S(1)}, f32[256,256]{1,0:T(8,128)}, u32[]{:S(2)}) copy-start(f32[256,256]{1,0:T(8,128)} %param.16) | copy-start | bytes 786436

commit v3 on v2

--- a/solution.py
+++ b/solution.py
@@ -24,7 +24,8 @@
     count_ref,
     h_ref,
     o_ref,
-    g_ref,
+    dt_ref,
+    low_ref,
     acc,
     total,
     hid,
@@ -34,6 +35,7 @@
     second,
     second_sum,
     third,
+    g_ref,
     hid_send,
     hid_recv,
     line_send,
@@ -192,8 +194,6 @@
     def _():
         line_copy(0, p).start()
 
-    for k in range(1, groups):
-        first_copy((e + k) % groups).start()
     sib_copy(p).start()
     hid_copy(sibling).start()
 
@@ -206,7 +206,21 @@
                 hid_copy(2 * q + c).start()
                 hid_copy(2 * q + 1 - c).start()
 
-    hid_start(1)
+    for k in range(chips - 1, 1, -1):
+        hid_start(k)
+
+    @pl.loop(0, g_ref.shape[0] // 256)
+    def _(i):
+        at = pl.ds(pl.multiple_of(i * 256, 256), 256)
+        g_ref[at, :] = lax.dot_general(
+            dt_ref[:, at],
+            low_ref[...],
+            (((0,), (0,)), ((), ())),
+            preferred_element_type=jnp.float32,
+        ).astype(jnp.bfloat16)
+
+    for k in range(1, groups):
+        first_copy((e + k) % groups).start()
 
     acc[...] = jnp.zeros_like(acc)
 
@@ -280,9 +294,9 @@
         def _():
             forward(k)
 
-            @pl.when(k < chips - 1)
+            @pl.when(k == 1)
             def _():
-                hid_start(k + 1)
+                hid_start(1)
 
         @pl.when(k == 1)
         def _():
@@ -321,12 +335,12 @@
         third_copy((p + k) % chips).wait_send()
 
 
-def gradients(n, groups, counts, hidden, out_rows, mamba_part):
+def gradients(n, groups, counts, hidden, out_rows, dt_grads, low_rank):
     capacity, total = hidden.shape
     width = out_rows.shape[1]
     cols = total // n
     chips = n // 2
-    inner, rank = mamba_part.shape
+    inner, rank = dt_grads.shape[1], low_rank.shape[1]
     block = inner // (n * groups)
     return pl.pallas_call(
         functools.partial(expert_kernel, n, groups),
@@ -337,6 +351,7 @@
         in_specs=[
             pl.BlockSpec(memory_space=pltpu.SMEM),
             pl.BlockSpec(memory_space=pl.ANY),
+            pl.BlockSpec(memory_space=pltpu.VMEM),
             pl.BlockSpec(memory_space=pltpu.VMEM),
             pl.BlockSpec(memory_space=pltpu.VMEM),
         ],
@@ -352,6 +367,7 @@
             pltpu.VMEM((chips, block, rank), jnp.bfloat16),
             pltpu.VMEM((chips, block, rank), jnp.bfloat16),
             pltpu.VMEM((chips, block, rank), jnp.bfloat16),
+            pltpu.VMEM((inner, rank), jnp.bfloat16),
             pltpu.SemaphoreType.DMA((n,)),
             pltpu.SemaphoreType.DMA((n,)),
             pltpu.SemaphoreType.DMA((2, chips)),
@@ -366,23 +382,19 @@
             pltpu.SemaphoreType.DMA((chips,)),
         ],
         compiler_params=pltpu.CompilerParams(
-            collective_id=0, has_side_effects=True, vmem_limit_bytes=52 * 2**20
+            collective_id=0, has_side_effects=True, vmem_limit_bytes=56 * 2**20
         ),
         cost_estimate=pl.CostEstimate(
             flops=2 * n * capacity * cols * width, bytes_accessed=600 * 2**20, transcendentals=0
         ),
-    )(counts, hidden, out_rows, mamba_part)
+    )(counts, hidden, out_rows, dt_grads, low_rank)
 
 
 def body(
     n, groups, hidden_rows, out_grads, counts, expert_m, expert_v, low_rank, dt_grads, mamba_m, mamba_v
 ):
-    contract = (((0,), (0,)), ((), ()))
-    mamba_part = lax.dot_general(
-        dt_grads, low_rank, contract, preferred_element_type=jnp.float32
-    ).astype(jnp.bfloat16)
     expert_grad, mamba_grad = gradients(
-        n, groups, counts, hidden_rows[0], out_grads[0], mamba_part
+        n, groups, counts, hidden_rows[0], out_grads[0], dt_grads, low_rank
     )
     moment_one, second, direction = adam_update(expert_m[0], expert_v[0], expert_grad)
     mamba_one, mamba_two, mamba_dir = adam_update(mamba_m, mamba_v, mamba_grad)

time: 290 us -> 253 us (0.87)
  Pallas kernels: 270 us -> 238 us
  matrix products: 5.51 us -> 0 us
    pallas_call x1, Pallas kernels: 270 us -> 238 us  [gradients(): pl.pallas_call(functools.partial(expert_kernel, n, groups), out_shape=(ja...]
    dot_general x1 -> x0, matrix products: 5.51 us -> none  [body(): lax.dot_general(dt_grads, low_rank, contract, preferred_element_type=jnp....]
where the time goes in v3:
time: 253 us
  Pallas kernels  238 us (94%)
  other arithmetic  12.9 us (5%)
    pallas_call x1, Pallas kernels, gradients(): pl.pallas_call(functools.partial(expert_kernel, n, groups), out_shape=(ja...  238 us
    broadcast_in_dim x1, other arithmetic, body(): direction.astype(jnp.bfloat16)[None]  12 us

profile of v3, /device:TPU:0, one launch (start us, length us, event | category | flops | bytes accessed | tf_op | source)
XLA Modules:
  0.0 252.8 jit_solution(10220968668687124408)
XLA Ops:
  1.3 0.0 copy-start
  1.3 238.5 %shard_map.136 = (f32[1024,2048]{1,0:T(8,128)}, f32[256,256]{1,0:T(8,128)}) custom-call(s32[1,1]{1,0:T(1,128)S(6)} %copy.15.count_ref, bf16[384,8192]{1,0:T(8,128)(2,1)} %bitcast.28, bf16[384,2048]{1,0:T(8,128)(2,1)} %bitcast.29, bf16[256,8192]{1,0:T(8,128)(2,1)} %dt_ref.1, bf16[256,256]{1,0:T(8,128)(2,1)} %low_ref.1), custom_call_target="tpu_custom_call" | custom-call | flops 12884901888 | bytes 629145600 | tf_op jit(solution)/shard_map/pallas_call | solution.py:345
  239.8 0.0 copy-done
  239.8 0.0 copy-start.1
  239.8 0.0 copy-start.2
  239.8 0.0 copy-start.3
  239.8 12.0 %fusion.5 = (bf16[1,1024,2048]{2,1,0:T(8,128)(2,1)}, bf16[1,1024,2048]{2,1,0:T(8,128)(2,1)}, bf16[1,1024,2048]{2,1,0:T(8,128)(2,1)}) fusion(f32[1024,2048]{1,0:T(8,128)} %get-tuple-element.8, bf16[1,1024,2048]{2,1,0:T(8,128)(2,1)S(1)} %copy-done, bf16[1,1024,2048]{2,1,0:T(8,128)(2,1)} %param.12), kind=kLoop, calls=%fused_computation.8 | loop fusion | flops 33554432 | bytes 29360128 | tf_op jit(solution)/shard_map/broadcast_in_dim | solution.py:404
  251.8 0.0 copy-done.1
  251.8 0.0 copy-done.2
  251.8 0.0 copy-done.3
  251.8 1.0 add_divide_fusion
Async XLA Ops:
  1.3 238.5 %copy-start = (bf16[1,1024,2048]{2,1,0:T(8,128)(2,1)S(1)}, bf16[1,1024,2048]{2,1,0:T(8,128)(2,1)}, u32[]{:S(2)}) copy-start(bf16[1,1024,2048]{2,1,0:T(8,128)(2,1)} %param.13) | copy-start | bytes 12582916
  239.8 12.0 %copy-start.1 = (f32[256,256]{1,0:T(8,128)S(1)}, f32[256,256]{1,0:T(8,128)}, u32[]{:S(2)}) copy-start(f32[256,256]{1,0:T(8,128)} %param.17) | copy-start | bytes 786436
  239.8 12.0 %copy-start.2 = (f32[256,256]{1,0:T(8,128)S(1)}, f32[256,256]{1,0:T(8,128)}, u32[]{:S(2)}) copy-start(f32[256,256]{1,0:T(8,128)} %param.16) | copy-start | bytes 786436
  239.8 12.0 %copy-start.3 = (f32[256,256]{1,0:T(8,128)S(1)}, f32[256,256]{1,0:T(8,128)}, u32[]{:S(2)}) copy-start(f32[256,256]{1,0:T(8,128)} %get-tuple-element.9) | copy-start | bytes 786436

commit v4 on v3

--- a/solution.py
+++ b/solution.py
@@ -75,13 +75,14 @@
         )
     pl.semaphore_wait(barrier, n + groups - 2)
 
-    def line_copy(side, q):
+    def line_copy(side, q, half):
         s = 2 * q + c
-        return pltpu.make_async_remote_copy(
-            src_ref=outs.at[s],
-            dst_ref=outs.at[s],
-            send_sem=line_send.at[side, q],
-            recv_sem=out_recv.at[s],
+        part = pl.ds(half * (capacity // 2), capacity // 2)
+        return pltpu.make_async_remote_copy(
+            src_ref=outs.at[s, part],
+            dst_ref=outs.at[s, part],
+            send_sem=line_send.at[side, q, half],
+            recv_sem=out_recv.at[half, s],
             device_id={"dp": d + (2 if side else -2)},
             device_id_type=MESH,
         )
@@ -92,13 +93,17 @@
             src_ref=outs.at[s],
             dst_ref=outs.at[s],
             send_sem=sib_send.at[q],
-            recv_sem=out_recv.at[s],
+            recv_sem=out_recv.at[0, s],
             device_id={"dp": sibling},
             device_id_type=MESH,
         )
 
     def out_arrival(s):
-        return pltpu.make_async_copy(outs.at[s], outs.at[s], out_recv.at[s])
+        return pltpu.make_async_copy(outs.at[s], outs.at[s], out_recv.at[0, s])
+
+    def half_arrival(s, half):
+        part = outs.at[s, pl.ds(half * (capacity // 2), capacity // 2)]
+        return pltpu.make_async_copy(part, part, out_recv.at[half, s])
 
     def hid_copy(t):
         return pltpu.make_async_remote_copy(
@@ -188,11 +193,13 @@
 
     @pl.when(p < chips - 1)
     def _():
-        line_copy(1, p).start()
+        line_copy(1, p, 0).start()
+        line_copy(1, p, 1).start()
 
     @pl.when(p > 0)
     def _():
-        line_copy(0, p).start()
+        line_copy(0, p, 0).start()
+        line_copy(0, p, 1).start()
 
     sib_copy(p).start()
     hid_copy(sibling).start()
@@ -247,21 +254,23 @@
 
         @pl.when(left >= 0)
         def _():
-            out_arrival(2 * left + c).wait()
-
-            @pl.when(p < chips - 1)
-            def _():
-                line_copy(1, left).start()
+            for half in range(2):
+                half_arrival(2 * left + c, half).wait()
+
+                @pl.when(p < chips - 1)
+                def _(half=half):
+                    line_copy(1, left, half).start()
 
             sib_copy(left).start()
 
         @pl.when(right < chips)
         def _():
-            out_arrival(2 * right + c).wait()
-
-            @pl.when(p > 0)
-            def _():
-                line_copy(0, right).start()
+            for half in range(2):
+                half_arrival(2 * right + c, half).wait()
+
+                @pl.when(p > 0)
+                def _(half=half):
+                    line_copy(0, right, half).start()
 
             sib_copy(right).start()
 
@@ -318,11 +327,13 @@
 
         @pl.when(jnp.logical_and(q <= p, p < chips - 1))
         def _():
-            line_copy(1, q).wait_send()
+            line_copy(1, q, 0).wait_send()
+            line_copy(1, q, 1).wait_send()
 
         @pl.when(jnp.logical_and(q >= p, p > 0))
         def _():
-            line_copy(0, q).wait_send()
+            line_copy(0, q, 0).wait_send()
+            line_copy(0, q, 1).wait_send()
 
     @pl.loop(1, n)
     def _(k):
@@ -370,9 +381,9 @@
             pltpu.VMEM((inner, rank), jnp.bfloat16),
             pltpu.SemaphoreType.DMA((n,)),
             pltpu.SemaphoreType.DMA((n,)),
-            pltpu.SemaphoreType.DMA((2, chips)),
+            pltpu.SemaphoreType.DMA((2, chips, 2)),
             pltpu.SemaphoreType.DMA((chips,)),
-            pltpu.SemaphoreType.DMA((n,)),
+            pltpu.SemaphoreType.DMA((2, n)),
             pltpu.SemaphoreType.DMA,
             pltpu.SemaphoreType.DMA((groups,)),
             pltpu.SemaphoreType.DMA((groups,)),

time: 253 us -> 249 us (0.984)
  Pallas kernels: 238 us -> 232 us
    pallas_call x1, Pallas kernels: 238 us -> 232 us  [gradients(): pl.pallas_call(functools.partial(expert_kernel, n, groups), out_shape=(ja...]
where the time goes in v4:
time: 249 us; the launch traced here: 247 us
  Pallas kernels  232 us (93%)
  other arithmetic  12.9 us (5%)
    pallas_call x1, Pallas kernels, gradients(): pl.pallas_call(functools.partial(expert_kernel, n, groups), out_shape=(ja...  232 us
    broadcast_in_dim x1, other arithmetic, body(): direction.astype(jnp.bfloat16)[None]  12 us

profile of v4, /device:TPU:0, one launch (start us, length us, event | category | flops | bytes accessed | tf_op | source)
XLA Modules:
  0.0 246.7 jit_solution(12986360438022278202)
XLA Ops:
  1.3 0.0 copy-start
  1.3 232.4 %shard_map.136 = (f32[1024,2048]{1,0:T(8,128)}, f32[256,256]{1,0:T(8,128)}) custom-call(s32[1,1]{1,0:T(1,128)S(6)} %copy.15.count_ref, bf16[384,8192]{1,0:T(8,128)(2,1)} %bitcast.28, bf16[384,2048]{1,0:T(8,128)(2,1)} %bitcast.29, bf16[256,8192]{1,0:T(8,128)(2,1)} %dt_ref.1, bf16[256,256]{1,0:T(8,128)(2,1)} %low_ref.1), custom_call_target="tpu_custom_call" | custom-call | flops 12884901888 | bytes 629145600 | tf_op jit(solution)/shard_map/pallas_call | solution.py:356
  233.7 0.0 copy-done
  233.7 0.0 copy-start.1
  233.7 0.0 copy-start.2
  233.7 0.0 copy-start.3
  233.7 12.0 %fusion.5 = (bf16[1,1024,2048]{2,1,0:T(8,128)(2,1)}, bf16[1,1024,2048]{2,1,0:T(8,128)(2,1)}, bf16[1,1024,2048]{2,1,0:T(8,128)(2,1)}) fusion(f32[1024,2048]{1,0:T(8,128)} %get-tuple-element.8, bf16[1,1024,2048]{2,1,0:T(8,128)(2,1)S(1)} %copy-done, bf16[1,1024,2048]{2,1,0:T(8,128)(2,1)} %param.12), kind=kLoop, calls=%fused_computation.8 | loop fusion | flops 33554432 | bytes 29360128 | tf_op jit(solution)/shard_map/broadcast_in_dim | solution.py:415
  245.7 0.0 copy-done.1
  245.7 0.0 copy-done.2
  245.7 0.0 copy-done.3
  245.7 1.0 add_divide_fusion
Async XLA Ops:
  1.3 232.4 %copy-start = (bf16[1,1024,2048]{2,1,0:T(8,128)(2,1)S(1)}, bf16[1,1024,2048]{2,1,0:T(8,128)(2,1)}, u32[]{:S(2)}) copy-start(bf16[1,1024,2048]{2,1,0:T(8,128)(2,1)} %param.13) | copy-start | bytes 12582916
  233.7 12.0 %copy-start.1 = (f32[256,256]{1,0:T(8,128)S(1)}, f32[256,256]{1,0:T(8,128)}, u32[]{:S(2)}) copy-start(f32[256,256]{1,0:T(8,128)} %param.17) | copy-start | bytes 786436
  233.7 12.0 %copy-start.2 = (f32[256,256]{1,0:T(8,128)S(1)}, f32[256,256]{1,0:T(8,128)}, u32[]{:S(2)}) copy-start(f32[256,256]{1,0:T(8,128)} %param.16) | copy-start | bytes 786436
  233.7 12.0 %copy-start.3 = (f32[256,256]{1,0:T(8,128)S(1)}, f32[256,256]{1,0:T(8,128)}, u32[]{:S(2)}) copy-start(f32[256,256]{1,0:T(8,128)} %get-tuple-element.9) | copy-start | bytes 786436
